TPU v7x, 256 devices: a whole 4x4x8 slice. The times are simulated.
256 devices in a mesh: dp: 32 (over z, y), mp: 8 (over x, core).
Axes of the slice: x: 4, y: 4, z: 8, core: 2. Of those that a mesh axis runs over, the one named last changes fastest.
Arguments:
- context: bfloat16 [64, 512, 3072], P('dp', None, 'mp'), may hold values from -0.625 to 0.625
- w_out: bfloat16 [3072, 6144], P('mp', 'dp'), may hold values from -0.109375 to 0.109375
- stream: bfloat16 [64, 512, 6144], P('dp', 'mp'), may hold values from -250 to 250
- gain: float32 [6144], replicated, may hold values from 0.1 to 1.9
- partner: int32 [64], replicated, may hold values from 0 to 63, as said below
Outputs:
- context_grad: bfloat16 [64, 512, 3072], P('dp', None, 'mp')
- weight_grad: float32 [3072, 6144], P('mp', 'dp')
- stream_grad: bfloat16 [64, 512, 6144], P('dp', 'mp')
Inputs may be any that keep to these rules, and one draw needn't show every extreme that they name: partner pairs the views: partner[partner[i]] = i and partner[i] != i; which views pair is drawn afresh.
All inputs are finite; a program needn't handle non-finite values.
Results may differ from a plain program's by a relative error of at most 0.004.
The roundings to bfloat16 on the way count: a program that leaves them out, or rounds other values in their place, can miss the bound.
Values may be sent and summed in bfloat16 or wider, within the bound.
A program may use at most 128 MiB of HBM per device.

v0:
```python
import jax
import jax.numpy as jnp
from jax import lax
from jax.sharding import PartitionSpec as P

EPS = 1e-06
SHARP = 10.0
LOSS_MUL = 512.0


def norm_scale(values):
    return lax.rsqrt(jnp.mean(values * values, axis=-1, keepdims=True) + EPS)


def stream_gradient(values, rstd, upstream):
    inner = jnp.mean(values * upstream[:, None, :], axis=-1, keepdims=True)
    return (rstd * upstream[:, None, :] - values * (rstd * rstd * rstd) * inner).astype(
        jnp.bfloat16
    )


def local(context, w_out, stream, gain, partner):
    emb_dev, seq_dev, width = stream.shape
    seq_all = context.shape[1]
    views = emb_dev * lax.axis_size("dp")
    first_view = lax.axis_index("dp") * emb_dev
    weights = lax.all_gather(w_out, "dp", axis=1, tiled=True)
    values = stream.astype(jnp.float32)
    rstd = norm_scale(values)
    pooled = lax.psum(jnp.sum(values * rstd * gain, axis=1), "mp") / seq_all
    inv = lax.rsqrt(jnp.sum(pooled * pooled, axis=-1, keepdims=True) + EPS)
    unit = pooled * inv
    emb = unit.astype(jnp.bfloat16)
    gathered = lax.all_gather(emb, "dp", axis=0, tiled=True)
    gathered_values = gathered.astype(jnp.float32)
    logits = SHARP * jnp.dot(emb, gathered.T, preferred_element_type=jnp.float32)
    own_index = first_view + jnp.arange(emb_dev, dtype=jnp.int32)
    all_index = jnp.arange(views, dtype=jnp.int32)
    diagonal = own_index[:, None] == all_index[None, :]
    expo = jnp.where(diagonal, jnp.float32(0.0), jnp.exp(logits))
    total = jnp.sum(expo, axis=1, keepdims=True)
    prob = expo / total
    own_partner = lax.dynamic_slice_in_dim(partner, first_view, emb_dev, 0)
    target = (own_partner[:, None] == all_index[None, :]).astype(jnp.float32)
    dlog = LOSS_MUL * (prob - target)
    row_side = SHARP * jnp.dot(dlog, gathered_values, precision=lax.Precision.HIGHEST)
    terms = SHARP * jnp.dot(dlog.T, emb.astype(jnp.float32), precision=lax.Precision.HIGHEST)
    column_side = lax.psum_scatter(terms, "dp", scatter_dimension=0, tiled=True)
    demb = row_side + column_side
    dpooled = inv * (demb - unit * jnp.sum(unit * demb, axis=-1, keepdims=True))
    upstream = gain * dpooled / seq_all
    stream_grad = stream_gradient(values, rstd, upstream)
    piece = lax.all_gather(stream_grad, "mp", axis=1, tiled=True)
    product = jnp.einsum("esd,hd->esh", piece, weights, preferred_element_type=jnp.float32)
    weight_acc = jnp.einsum("esh,esd->hd", context, piece, preferred_element_type=jnp.float32)
    weight_grad = lax.psum_scatter(weight_acc, "dp", scatter_dimension=1, tiled=True)
    return (product.astype(jnp.bfloat16), weight_grad, stream_grad)


def solution(mesh):
    placed = (P("dp", None, "mp"), P("mp", "dp"), P("dp", "mp", None), P(), P())
    return jax.shard_map(
        local,
        mesh=mesh,
        in_specs=placed,
        out_specs=(P("dp", None, "mp"), P("mp", "dp"), P("dp", "mp", None)),
        check_vma=False,
    )
```

profile of v0, /device:TPU:8, one launch (start us, length us, event | category | flops | bytes accessed | tf_op | source)
XLA Modules:
  0.0 644.7 jit_solution(15189100127399530242)
XLA Ops:
  7.2 0.0 copy-start
  7.2 0.0 all-reduce.3.cloned.1.call-start
  7.2 0.0 copy-start.3
  7.2 1.9 fusion.3
  9.1 2.0 fusion.5
  11.1 26.1 %psum.7 = f32[2,6144]{1,0:T(2,128)S(1)} all-reduce(f32[2,6144]{1,0:T(2,128)S(1)} %fusion.5), channel_id=1, replica_groups=mesh['dp'=32,'mp'=8] {'mp'}, use_global_device_ids=true, to_apply=%region_2.0 | all-reduce | flops 12288 | bytes 98304 | tf_op jit(solution)/shard_map/psum | solution.py:30
  37.2 0.2 multiply_reduce_fusion.1
  37.4 0.1 fusion.26
  37.5 0.0 copy-start.4
  37.5 57.0 %all-gather = bf16[32,2,6144]{2,1,0:T(2,128)(2,1)} all-gather(bf16[1,2,6144]{2,1,0:T(2,128)(2,1)S(1)} %fusion.26), channel_id=1, replica_groups=mesh['dp'=32,'mp'=8] {'dp'}, dimensions={0}, use_global_device_ids=true | all-gather | bytes 811008 | tf_op jit(solution)/shard_map/all_gather | solution.py:34
  94.5 2.4 reshape.41
  97.0 0.5 fusion.18
  97.4 0.1 dynamic_slice.3
  97.5 2.1 convolution_multiply_fusion
  99.6 0.0 all-reduce.3.cloned.1.call-update
  99.6 0.0 all-gather.4.cloned.1.call-start
  99.7 0.6 dynamic-slice
  100.9 145.0 %all-reduce.3.cloned.1.call-done = f32[64,6144]{1,0:T(8,128)} async-done(((f32[64,6144]{1,0:T(8,128)}), f32[64,6144]{1,0:T(8,128)}) %all-reduce.3.cloned.1.call-update) | async-done | bytes 1572880
  245.9 1.5 multiply_reduce_fusion
  247.4 0.1 multiply_multiply_fusion
  247.6 0.4 fusion.9
  248.0 1.9 fusion.8
  249.9 0.0 all-gather.4.cloned.1.call-update
  249.9 0.0 all-gather.6.cloned.1.call-start
  249.9 0.7 all-gather.6.cloned.1.call-update
  250.6 0.0 reduce-scatter.2.cloned.1.call-start
  250.7 67.6 %all-gather.4.cloned.1.call-done = bf16[2,512,6144]{2,1,0:T(8,128)(2,1)} async-done(((bf16[2,64,6144]{2,1,0:T(8,128)(2,1)}), bf16[2,512,6144]{2,1,0:T(8,128)(2,1)}) %all-gather.4.cloned.1.call-update) | async-done | bytes 12582928 | tf_op jit(solution)/shard_map/all_gather | solution.py:53
  318.3 11.9 %convolution_bitcast_fusion = f32[384,6144]{0,1:T(8,128)} fusion(bf16[2,512,6144]{2,1,0:T(8,128)(2,1)} %all-gather.4.cloned.1.call-done, bf16[2,512,384]{2,1,0:T(8,128)(2,1)S(1)} %copy-done), kind=kOutput, calls=%fused_computation | convolution fusion | flops 4831838208 | bytes 22806528 | tf_op jit(solution)/shard_map/esh,esd->hd/dot_general | solution.py:55
  330.2 0.0 reduce-scatter.2.cloned.1.call-update
  330.2 73.8 %all-gather.6.cloned.1.call-done = bf16[384,6144]{0,1:T(8,128)(2,1)} async-done(((bf16[384,192]{0,1:T(8,128)(2,1)}), bf16[384,6144]{0,1:T(8,128)(2,1)}) %all-gather.6.cloned.1.call-update) | async-done | bytes 4718608 | tf_op jit(solution)/shard_map/all_gather | solution.py:27
  404.0 11.7 %fusion.10 = bf16[2,512,384]{2,1,0:T(8,128)(2,1)} fusion(bf16[2,512,6144]{2,1,0:T(8,128)(2,1)} %all-gather.4.cloned.1.call-done, bf16[384,6144]{0,1:T(8,128)(2,1)} %all-gather.6.cloned.1.call-done), kind=kOutput, calls=%fused_computation.17 | convolution fusion | flops 4832231424 | bytes 18087936 | tf_op jit(solution)/shard_map/esd,hd->esh/dot_general | solution.py:54
  415.7 222.5 %reduce-scatter.2.cloned.1.call-done = f32[384,192]{0,1:T(8,128)} async-done(((f32[384,6144]{0,1:T(8,128)}), f32[384,192]{0,1:T(8,128)}) %reduce-scatter.2.cloned.1.call-update) | async-done | bytes 294928 | tf_op jit(solution)/shard_map/reduce_scatter | solution.py:56
  (11 shorter events, 0.0 us)
Async XLA Ops:
  7.2 311.1 %copy-start = (bf16[2,512,384]{2,1,0:T(8,128)(2,1)S(1)}, bf16[2,512,384]{2,1,0:T(8,128)(2,1)}, u32[]{:S(2)}) copy-start(bf16[2,512,384]{2,1,0:T(8,128)(2,1)} %param.5) | copy-start | bytes 2359300
  7.2 238.7 %all-reduce.3.cloned.1.call-start = ((), (), s32[]{:S(2)}) async-start(), calls=%async_computation.4 | async-start | bytes 3145728
  7.2 90.2 %copy-start.3 = (s32[64]{0:T(128)S(1)}, s32[64]{0:T(128)}, u32[]{:S(2)}) copy-start(s32[64]{0:T(128)} %param.9) | copy-start | bytes 772
  37.5 62.2 %copy-start.4 = (u32[256]{0:T(256)S(1)}, u32[256]{0:T(256)}, u32[]{:S(2)}) copy-start(u32[256]{0:T(256)} %constant.35) | copy-start | bytes 3076
  94.5 152.9 %copy-start.2 = (f32[6144]{0:T(1024)S(1)}, f32[6144]{0:T(1024)}, u32[]{:S(2)}) copy-start(f32[6144]{0:T(1024)} %param.8) | copy-start | bytes 73732
  94.5 153.0 %copy-start.1 = (bf16[2,64,6144]{2,1,0:T(8,128)(2,1)S(1)}, bf16[2,64,6144]{2,1,0:T(8,128)(2,1)}, u32[]{:S(2)}) copy-start(bf16[2,64,6144]{2,1,0:T(8,128)(2,1)} %param.7) | copy-start | bytes 4718596
  99.6 218.6 %all-gather.4.cloned.1.call-start = ((), (), s32[]{:S(2)}) async-start(), calls=%async_computation.1 | async-start | bytes 14155776 | tf_op jit(solution)/shard_map/all_gather | solution.py:53
  249.9 154.1 %all-gather.6.cloned.1.call-start = ((), (), s32[]{:S(2)}) async-start(), calls=%async_computation.2 | async-start | bytes 4866048 | tf_op jit(solution)/shard_map/all_gather | solution.py:27
  250.6 387.6 %reduce-scatter.2.cloned.1.call-start = ((), (), s32[]{:S(2)}) async-start(), calls=%async_computation.3 | async-start | bytes 9732096 | tf_op jit(solution)/shard_map/reduce_scatter | solution.py:56
Sparse Core Ops, SparseCore 0:
  99.7 146.1 all-reduce.2
  250.0 68.2 all-gather.3
  321.2 82.7 all-gather.5
  409.0 229.1 reduce-scatter.1
where the time goes:
time: 646 us; the launch traced here: 645 us
  waiting for transfers between devices  510 us (79%)
  blocking collectives  83.1 us (13%)
  matrix products  27.7 us (4%)
  between operations  14.5 us (2%)
  other arithmetic  6.58 us (1%)
    reduce_scatter x1, waiting for transfers between devices, local(): lax.psum_scatter(weight_acc, 'dp', scatter_dimension=1, tiled=True)  222 us
    unnamed x5, waiting for transfers between devices  146 us
    all_gather x1, waiting for transfers between devices, local(): weights = lax.all_gather(w_out, 'dp', axis=1, tiled=True)  73.8 us
    all_gather x1, waiting for transfers between devices, local(): piece = lax.all_gather(stream_grad, 'mp', axis=1, tiled=True)  67.6 us
    all_gather x1, blocking collectives, local(): gathered = lax.all_gather(emb, 'dp', axis=0, tiled=True)  57 us
    psum x1, blocking collectives, local(): pooled = lax.psum(jnp.sum(values * rstd * gain, axis=1), 'mp') / seq_all  26.1 us
  transfers between devices with their start and end apart: 4, of which 4 were waited for; matrix products, arithmetic and copies ran while one was open for 4% of the time, Pallas kernels for 0%

commit v1 on v0

v1 whole, which is shorter than its diff:
```python
import jax
import jax.numpy as jnp
from jax import lax
from jax.experimental import pallas as pl
from jax.experimental.pallas import tpu as pltpu
from jax.sharding import PartitionSpec as P

EPS = 1e-06
SHARP = 10.0
LOSS_MUL = 512.0
D = 6144
SEQ = 512
HEADS = 384
VIEWS = 64
NZ, NY, NX = 8, 4, 4
MP = 8
OWN = 64
BLK = 768
PART = 192
HALF = PART // 2
PAY = PART + 16
PAYH = HALF + 16
F32 = jnp.float32
BF16 = jnp.bfloat16
I16 = jnp.int16
HIGH = lax.Precision.HIGHEST


def encode(values):
    top = jnp.max(jnp.abs(values), axis=0, keepdims=True)
    expo = jnp.ceil(16.0 * jnp.log2(jnp.maximum(top, 1e-30)))
    whole = jnp.round(values * jnp.exp2(14.9 - expo * 0.0625)).astype(jnp.int32).astype(I16)
    tail = jnp.broadcast_to(expo, (16, HEADS)).astype(jnp.int32).astype(I16)
    return whole, tail


def decode(ref, rows):
    expo = ref[pl.ds(rows, 16), :].astype(jnp.int32).astype(F32)[0:1, :]
    return ref[pl.ds(0, rows), :].astype(jnp.int32).astype(F32) * jnp.exp2(expo * 0.0625 - 14.9)


def put(ref, values, rows):
    whole, tail = encode(values)
    ref[pl.ds(0, rows), :] = whole
    ref[pl.ds(rows, 16), :] = tail


def kernel(
    ctx_hbm, w_hbm, stream_hbm, gain_ref, partner_ref,
    cg_hbm, wg_hbm, sg_hbm,
    G, SG, WT, CTX, CG, CGO, PB, WGO,
    EX1, UN, YB, ZB, E, LB, UPM, UPF, TM, TT, RB, CB,
    YS0, YR0, YS1, YR1, ZS0, ZR0, ZS1, ZR1,
    in_sem, out_sem, sgo_sem,
    xs_s, x_r, wy_s, wy_r, wz_s, wz_r,
    e1_s, e1_r, ey_s, ey_r, ez_s, ez_r, el_s, el_r, eu_s, eu_r, et_s, et_r,
    ys0_s, ys0_r, ys1_s, ys1_r, zs0_s, zs0_r, zs1_s, zs1_r,
):
    dp = lax.axis_index("dp")
    mp = lax.axis_index("mp")
    z, y = lax.div(dp, NY), lax.rem(dp, NY)
    x, core = lax.div(mp, 2), lax.rem(mp, 2)

    def zy(dz, dy):
        return lax.rem(z + (dz + NZ), NZ) * NY + lax.rem(y + (dy + NY), NY)

    def slot(dx, other):
        c = 1 - core if other else core
        return lax.rem(x + (dx + NX), NX) * 2 + c

    def near(dx=0, other=False, dz=0, dy=0):
        return (zy(dz, dy), slot(dx, other))

    def remote(src, dst, ss, rs, dev):
        return pltpu.make_async_remote_copy(
            src_ref=src, dst_ref=dst, send_sem=ss, recv_sem=rs,
            device_id=dev, device_id_type=pl.DeviceIdType.MESH,
        )

    own_rows = pl.ds(pl.multiple_of(mp * OWN, OWN), OWN)
    load_stream = pltpu.make_async_copy(stream_hbm, G.at[:, own_rows, :], in_sem.at[0])
    load_ctx = pltpu.make_async_copy(ctx_hbm, CTX, in_sem.at[1])
    load_w = pltpu.make_async_copy(
        w_hbm, WT.at[pl.ds(pl.multiple_of(dp * PART, PART), PART), :], in_sem.at[2]
    )
    load_stream.start()
    load_w.start()
    load_ctx.start()

    barrier = pltpu.get_barrier_semaphore()
    peers = [(dp, lax.rem(mp + d, MP)) for d in range(1, MP)]
    ypeers = [near(dy=d) for d in range(1, NY)]
    zpeers = [near(dz=d) for d in range(1, NZ)]
    for dev in peers + ypeers + zpeers:
        pl.semaphore_signal(barrier, inc=1, device_id=dev, device_id_type=pl.DeviceIdType.MESH)

    def zblock(k):
        dist = lax.div(NZ - k, 2)
        odd = lax.rem(k, 2)
        return lax.rem(z + NZ + (2 * odd - 1) * dist, NZ)

    def cols(k):
        return pl.ds(pl.multiple_of(zblock(k) * BLK, BLK), BLK)

    def rows(s):
        return pl.ds(pl.multiple_of(s * OWN, OWN), OWN)

    def x_own(k, t):
        ref = G.at[:, own_rows, cols(k)]
        dev = (near(dx=1), near(dx=-1), near(other=True))[t]
        return remote(ref, ref, xs_s.at[k, t], x_r.at[k, t], dev)

    def x_fwd(k, t):
        if t == 0:
            ref = G.at[0, rows(slot(-1, False)), cols(k)]
            return remote(ref, ref, xs_s.at[k, 3], x_r.at[k, 3], near(dx=1))
        ref = G.at[1, rows(slot(1, False)), cols(k)]
        return remote(ref, ref, xs_s.at[k, 4], x_r.at[k, 4], near(dx=-1))

    def x_sib(k, t):
        ref = G.at[:, rows(slot((-1, 1, 2)[t], False)), cols(k)]
        return remote(ref, ref, xs_s.at[k, 5 + t], x_r.at[k, 5 + t], near(other=True))

    def x_wait(k, t):
        if t < 3:
            ref = G.at[:, rows((slot(-1, False), slot(1, False), slot(0, True))[t]), cols(k)]
        elif t < 5:
            ref = G.at[t - 3, rows(slot(2, False)), cols(k)]
        else:
            ref = G.at[:, rows(slot((-1, 1, 2)[t - 5], True)), cols(k)]
        remote(ref, ref, xs_s.at[k, t], x_r.at[k, t], near(other=True)).wait_recv()

    def x_send(k):
        for t in range(3):
            x_own(k, t).start()

    def x_forward(k):
        x_wait(k, 0)
        x_fwd(k, 0).start()
        x_sib(k, 0).start()
        x_wait(k, 1)
        x_fwd(k, 1).start()
        x_sib(k, 1).start()

    def x_opposite(k):
        x_wait(k, 3)
        x_wait(k, 4)
        x_sib(k, 2).start()

    def x_arrived(k):
        x_wait(k, 2)
        for t in (5, 6, 7):
            x_wait(k, t)

    def wy_copy(d):
        ref = WT.at[pl.ds(pl.multiple_of(dp * PART, PART), PART), :]
        return remote(ref, ref, wy_s.at[d - 1], wy_r.at[y], near(dy=d))

    def wy_wait(d):
        s = lax.rem(y + d, NY)
        ref = WT.at[pl.ds(pl.multiple_of((z * NY + s) * PART, PART), PART), :]
        remote(ref, ref, wy_s.at[d - 1], wy_r.at[s], near(dy=d)).wait_recv()

    def wz_ref(bundle, f, t):
        start = pl.multiple_of(bundle * BLK, BLK)
        if f == 3:
            return WT.at[pl.ds(pl.multiple_of(start + t * (BLK // 2), BLK // 2), BLK // 2), :]
        return WT.at[pl.ds(start, BLK), :]

    def wz_copy(f, t):
        step = f if t else NZ - f
        ref = wz_ref(lax.rem(z + step, NZ), f, t)
        return remote(ref, ref, wz_s.at[f, t], wz_r.at[f, t], near(dz=-1 if t else 1))

    def wz_wait(f, t):
        step = f + 1 if t else NZ - f - 1
        ref = wz_ref(lax.rem(z + step, NZ), f, t)
        remote(ref, ref, wz_s.at[f, t], wz_r.at[f, t], near(dz=1)).wait_recv()

    def wz_next(f):
        for t in range(2):
            wz_wait(f - 1, t)
            wz_copy(f, t).start()

    def ex(buf, ss, rs, d):
        ref = buf.at[mp]
        return remote(ref, ref, ss.at[d - 1], rs.at[mp], (dp, lax.rem(mp + d, MP)))

    def ex_send(buf, ss, rs):
        for d in (4, 2, 3, 5, 6, 7, 1):
            ex(buf, ss, rs, d).start()

    def ex_wait(buf, ss, rs):
        for d in range(1, MP):
            s = lax.rem(mp + d, MP)
            ref = buf.at[s]
            remote(ref, ref, ss.at[d - 1], rs.at[s], (dp, s)).wait_recv()

    def ey_copy(d):
        ref = YB.at[y]
        return remote(ref, ref, ey_s.at[d - 1], ey_r.at[y], near(dy=d))

    def ez_copy(d):
        ref = ZB.at[z]
        return remote(ref, ref, ez_s.at[d - 1], ez_r.at[z], near(dz=d))

    load_stream.wait()

    def rstd_of(v):
        acc = jnp.zeros((OWN, 128), F32)
        for q in range(D // 128):
            part = G[v, own_rows, pl.ds(q * 128, 128)].astype(F32)
            acc = acc + part * part
        mean = jnp.sum(acc, axis=1, keepdims=True) * (1.0 / D)
        return lax.rsqrt(mean + EPS)

    rstd = [rstd_of(v) for v in range(2)]
    for v in range(2):
        for q in range(MP):
            part = G[v, own_rows, pl.ds(q * BLK, BLK)].astype(F32)
            EX1[mp, v, pl.ds(q, 1), :] = jnp.sum(part * rstd[v], axis=0, keepdims=True)

    pl.semaphore_wait(barrier, (MP - 1) + (NY - 1) + (NZ - 1))
    ex_send(EX1, e1_s, e1_r)
    load_w.wait()
    for d in (2, 1, 3):
        wy_copy(d).start()
    x_send(0)
    x_send(1)
    ex_wait(EX1, e1_s, e1_r)

    gain8 = gain_ref[...]
    squares = []
    for v in range(2):
        total = EX1[0, v]
        for s in range(1, MP):
            total = total + EX1[s, v]
        pooled = total * gain8 * (1.0 / SEQ)
        UN[v] = pooled
        sq = jnp.sum(jnp.sum(pooled * pooled, axis=1, keepdims=True), axis=0, keepdims=True)
        squares.append(lax.rsqrt(sq + EPS))
    unit = [UN[v, pl.ds(mp, 1), :] * squares[v] for v in range(2)]
    emb = [u.astype(BF16).astype(F32) for u in unit]
    row8 = lax.broadcasted_iota(jnp.int32, (8, BLK), 0)
    zero8 = jnp.zeros((8, BLK), F32)

    def two(a, b, first):
        return jnp.where(row8 == first, a, jnp.where(row8 == first + 1, b, zero8))

    YB[y] = two(emb[0], emb[1], 2 * y)
    for d in (2, 1, 3):
        ey_copy(d).start()
    unit8 = two(unit[0], unit[1], 0)
    for d in range(1, NY):
        s = lax.rem(y + d, NY)
        ref = YB.at[s]
        remote(ref, ref, ey_s.at[d - 1], ey_r.at[s], near(dy=d)).wait_recv()
    eight = YB[0] + YB[1] + YB[2] + YB[3]
    ZB[z] = jnp.concatenate([eight[:, 0:HEADS], eight[:, HEADS:BLK]], axis=0).astype(BF16)
    for d in (4, 3, 5, 2, 6, 1, 7):
        ez_copy(d).start()
    for d in range(1, NY):
        wy_wait(d)
    for t in range(2):
        wz_copy(0, t).start()
    x_send(2)
    for d in range(1, NZ):
        s = lax.rem(z + d, NZ)
        ref = ZB.at[s]
        remote(ref, ref, ez_s.at[d - 1], ez_r.at[s], near(dz=d)).wait_recv()
    for s in range(NZ):
        part = ZB[s].astype(F32)
        E[pl.ds(8 * s, 8), pl.ds(0, HEADS)] = part[0:8]
        E[pl.ds(8 * s, 8), pl.ds(HEADS, HEADS)] = part[8:16]

    every = E[...]
    small = every.astype(BF16)
    contract = (((1,), (1,)), ((), ()))
    raw = lax.dot_general(small, small, contract, preferred_element_type=F32)
    cross = lax.dot_general(unit8, every, contract, precision=HIGH, preferred_element_type=F32)
    LB[mp, pl.ds(0, 32), pl.ds(0, 64)] = raw[0:32]
    LB[mp, pl.ds(0, 32), pl.ds(64, 64)] = raw[32:64]
    LB[mp, pl.ds(32, 8), pl.ds(0, 64)] = cross
    LB[mp, pl.ds(32, 8), pl.ds(64, 64)] = jnp.zeros((8, 64), F32)
    ex_send(LB, el_s, el_r)
    x_forward(0)
    x_send(3)
    ex_wait(LB, el_s, el_r)
    summed = LB[0]
    for s in range(1, MP):
        summed = summed + LB[s]
    logits = SHARP * jnp.concatenate([summed[0:32, 0:64], summed[0:32, 64:128]], axis=0)
    cross = summed[32:40, 0:64]

    rowi = lax.broadcasted_iota(jnp.int32, (VIEWS, VIEWS), 0)
    coli = lax.broadcasted_iota(jnp.int32, (VIEWS, VIEWS), 1)
    expo = jnp.where(rowi == coli, jnp.float32(0.0), jnp.exp(logits))
    both = expo / jnp.sum(expo, axis=1, keepdims=True) + expo / jnp.sum(expo, axis=0, keepdims=True)
    lane = lax.broadcasted_iota(jnp.int32, (1, VIEWS), 1)
    coef = []
    for v in range(2):
        index = 2 * dp + v
        mine = jnp.sum(jnp.where(rowi == index, both, 0.0), axis=0, keepdims=True)
        target = jnp.where(lane == partner_ref[index], jnp.float32(2.0), jnp.float32(0.0))
        coef.append(LOSS_MUL * (mine - target))
    r64 = lax.broadcasted_iota(jnp.int32, (8, VIEWS), 0)
    coef8 = jnp.where(r64 == 0, coef[0], jnp.where(r64 == 1, coef[1], jnp.zeros((8, VIEWS), F32)))
    demb = SHARP * jnp.dot(coef8, every, precision=HIGH, preferred_element_type=F32)
    along = SHARP * jnp.sum(coef8 * cross, axis=1, keepdims=True)
    inv8 = two(jnp.broadcast_to(squares[0], (1, BLK)), jnp.broadcast_to(squares[1], (1, BLK)), 0)
    dpooled = inv8 * (demb - unit8 * along)
    up8 = gain_ref[pl.ds(mp, 1), :] * dpooled * (1.0 / SEQ)
    UPM[mp] = jnp.zeros((8, 256), F32)
    for v in range(2):
        for c in range(3):
            UPM[mp, pl.ds(3 * v + c, 1), :] = up8[v : v + 1, 256 * c : 256 * (c + 1)]
    ex_send(UPM, eu_s, eu_r)
    x_opposite(0)
    x_forward(1)
    x_send(4)
    ex_wait(UPM, eu_s, eu_r)
    for s in range(MP):
        for v in range(2):
            for c in range(3):
                UPF[v, :, pl.ds(s * BLK + 256 * c, 256)] = UPM[s, pl.ds(3 * v + c, 1), :]

    diag = lax.broadcasted_iota(jnp.int32, (OWN, OWN), 0) == lax.broadcasted_iota(jnp.int32, (OWN, OWN), 1)
    TM[mp] = jnp.zeros((8, 128), F32)
    for v in range(2):
        acc = jnp.zeros((OWN, 128), F32)
        for q in range(D // 128):
            part = G[v, own_rows, pl.ds(q * 128, 128)].astype(F32)
            acc = acc + part * UPF[v, :, pl.ds(q * 128, 128)]
        inner = jnp.sum(acc, axis=1, keepdims=True) * (1.0 / D)
        slope = rstd[v] * rstd[v] * rstd[v] * inner
        for r, column in enumerate((rstd[v], slope)):
            line = jnp.sum(jnp.where(diag, column, 0.0), axis=0, keepdims=True)
            TM[mp, pl.ds(r, 1), pl.ds(v * OWN, OWN)] = line
    ex_send(TM, et_s, et_r)
    load_ctx.wait()
    CG[...] = jnp.zeros_like(CG)
    ex_wait(TM, et_s, et_r)
    for s in range(MP):
        TT[pl.ds(8 * s, 8), :] = TM[s]
    TT[pl.ds(64, 64), :] = jnp.zeros((64, 128), F32)
    flat = TT[...].T
    for s in range(MP):
        for v in range(2):
            piece = flat[v * OWN : (v + 1) * OWN]
            RB[v, pl.ds(s * OWN, OWN), :] = jnp.broadcast_to(piece[:, 8 * s : 8 * s + 1], (OWN, 128))
            CB[v, pl.ds(s * OWN, OWN), :] = jnp.broadcast_to(piece[:, 8 * s + 1 : 8 * s + 2], (OWN, 128))

    def part_rows(dy):
        return pl.ds(pl.multiple_of(lax.rem(y + dy, NY) * PART, PART), PART)

    def half_rows(dy, h):
        start = lax.rem(y + dy, NY) * PART + h * HALF
        return pl.ds(pl.multiple_of(start, HALF), HALF)

    def ys0(k, h):
        return remote(YS0.at[k, h], YR0.at[k, h], ys0_s.at[k, h], ys0_r.at[k, h], near(dy=1 if h == 0 else -1))

    def ys1(k, h):
        return remote(YS1.at[k, h], YR1.at[k, h], ys1_s.at[k, h], ys1_r.at[k, h], near(dy=1 if h == 0 else -1))

    def zs0(h):
        return remote(ZS0.at[h], ZR0.at[h], zs0_s.at[h], zs0_r.at[h], near(dz=1 if h == 0 else -1))

    def zs1(k):
        odd = lax.rem(k, 2)
        target = lax.rem(z + NZ - 1 + 2 * odd, NZ) * NY + y
        return remote(ZS1.at[k], ZR1.at[k], zs1_s.at[k], zs1_r.at[k], (target, mp))

    def sgout(k):
        return pltpu.make_async_copy(SG.at[:, own_rows, cols(k)], sg_hbm.at[:, :, cols(k)], sgo_sem.at[k])

    def block(k):
        first = zblock(k) * BLK
        x_arrived(k)

        def build(g, carry):
            v = lax.div(g, MP)
            r = rows(lax.rem(g, MP))
            rs = RB[v, r, :]
            cs = CB[v, r, :]
            for l in range(BLK // 128):
                c = pl.ds(pl.multiple_of(first + l * 128, 128), 128)
                value = G[v, r, c].astype(F32)
                SG[v, r, c] = (rs * UPF[v, :, c] - value * cs).astype(BF16)
            return carry

        lax.fori_loop(0, 2 * MP, build, 0)
        sgout(k).start()
        keep = lax.rem(k, 3)

        def matmul(m, carry):
            c = pl.ds(pl.multiple_of(first + m * 256, 256), 256)
            left = SG[:, :, c].reshape(2 * SEQ, 256)
            right = CTX[...].reshape(2 * SEQ, HEADS)
            PB[keep, pl.ds(pl.multiple_of(m * 256, 256), 256), :] = lax.dot_general(
                left, right, (((0,), (0,)), ((), ())), preferred_element_type=F32
            )
            return carry

        lax.fori_loop(0, 3, matmul, 0)
        for h in range(2):
            put(YS0.at[k, h], PB[keep, half_rows(2, h), :], HALF)
            ys0(k, h).start()

    def y_second(k):
        keep = lax.rem(k, 3)
        for h in range(2):
            ys0(k, h).wait_recv()
            spot = half_rows(1 if h == 0 else 3, h)
            PB[keep, spot, :] = PB[keep, spot, :] + decode(YR0.at[k, h], HALF)
            put(YS1.at[k, h], PB[keep, part_rows(1 if h == 0 else 3), :], PART)
            ys1(k, h).start()

    def z_part(k):
        keep = lax.rem(k, 3)
        ys1(k, 0).wait_recv()
        ys1(k, 1).wait_recv()
        spot = part_rows(0)
        PB[keep, spot, :] = PB[keep, spot, :] + decode(YR1.at[k, 0], PART) + decode(YR1.at[k, 1], PART)

        @pl.when(k == 0)
        def _():
            for h in range(2):
                put(ZS0.at[h], PB[keep, half_rows(0, h), :], HALF)
                zs0(h).start()

        for h in range(2):
            @pl.when(k == 1 + h)
            def _():
                zs0(h).wait_recv()
                half = half_rows(0, h)
                PB[keep, half, :] = PB[keep, half, :] + decode(ZR0.at[h], HALF)

        @pl.when(jnp.logical_and(k >= 3, k <= 6))
        def _():
            zs1(k - 2).wait_recv()
            PB[keep, spot, :] = PB[keep, spot, :] + decode(ZR1.at[k - 2], PART)

        @pl.when(jnp.logical_and(k >= 1, k <= 6))
        def _():
            put(ZS1.at[k], PB[keep, spot, :], PART)
            zs1(k).start()

        @pl.when(k == 7)
        def _():
            zs1(5).wait_recv()
            zs1(6).wait_recv()
            WGO[...] = PB[keep, spot, :] + decode(ZR1.at[5], PART) + decode(ZR1.at[6], PART)

    def project(b):
        first = zblock(b) * BLK

        def step(m, carry):
            v = lax.div(m, 2)
            r = pl.ds(pl.multiple_of(lax.rem(m, 2) * 256, 256), 256)
            left = SG[v, r, pl.ds(pl.multiple_of(first, BLK), BLK)]
            right = WT[pl.ds(pl.multiple_of(first, BLK), BLK), :]
            CG[v, r, :] = CG[v, r, :] + jnp.dot(left, right, preferred_element_type=F32)
            return carry

        lax.fori_loop(0, 4, step, 0)

    def iteration(k, carry):
        @pl.when(k <= 2)
        def _():
            x_send(k + 5)

        @pl.when(k <= 5)
        def _():
            x_forward(k + 2)

        @pl.when(k <= 6)
        def _():
            x_opposite(k + 1)

        for f in range(1, 4):
            @pl.when(k == 2 * f - 2)
            def _():
                wz_next(f)

        @pl.when(k <= 7)
        def _():
            block(k)

        @pl.when(jnp.logical_and(k >= 1, k <= 8))
        def _():
            y_second(k - 1)

        @pl.when(k >= 2)
        def _():
            z_part(k - 2)

        @pl.when(jnp.logical_and(k >= 4, k <= 5))
        def _():
            project(k - 1)

        @pl.when(jnp.logical_and(k >= 6, k <= 7))
        def _():
            project(k - 5)

        @pl.when(k == 8)
        def _():
            project(5)
            project(6)
            project(7)
            wz_wait(3, 0)
            wz_wait(3, 1)
            project(0)
            CGO[...] = CG[...].astype(BF16)
            pltpu.make_async_copy(CGO, cg_hbm, out_sem.at[0]).start()

        return carry

    lax.fori_loop(0, 10, iteration, 0)
    wg_out = pltpu.make_async_copy(WGO, wg_hbm, out_sem.at[1])
    wg_out.start()

    def drain(k, carry):
        for t in range(3):
            x_own(k, t).wait_send()
            x_sib(k, t).wait_send()
        for h in range(2):
            x_fwd(k, h).wait_send()
            ys0(k, h).wait_send()
            ys1(k, h).wait_send()
        sgout(k).wait()

        @pl.when(jnp.logical_and(k >= 1, k <= 6))
        def _():
            zs1(k).wait_send()

        return carry

    lax.fori_loop(0, NZ, drain, 0)
    for h in range(2):
        zs0(h).wait_send()
    for d in range(1, NY):
        wy_copy(d).wait_send()
        ey_copy(d).wait_send()
    for f in range(4):
        for t in range(2):
            wz_copy(f, t).wait_send()
    for d in range(1, NZ):
        ez_copy(d).wait_send()
    for d in range(1, MP):
        ex(EX1, e1_s, e1_r, d).wait_send()
        ex(LB, el_s, el_r, d).wait_send()
        ex(UPM, eu_s, eu_r, d).wait_send()
        ex(TM, et_s, et_r, d).wait_send()
    pltpu.make_async_copy(CGO, cg_hbm, out_sem.at[0]).wait()
    wg_out.wait()


def local(context, w_out, stream, gain, partner):
    anywhere = pl.BlockSpec(memory_space=pl.ANY)
    sems = pltpu.SemaphoreType.DMA
    vm = pltpu.VMEM
    scratch = [
        vm((2, SEQ, D), BF16), vm((2, SEQ, D), BF16), vm((D, HEADS), BF16), vm((2, SEQ, HEADS), BF16),
        vm((2, SEQ, HEADS), F32), vm((2, SEQ, HEADS), BF16), vm((3, BLK, HEADS), F32), vm((PART, HEADS), F32),
        vm((MP, 2, MP, BLK), F32), vm((2, MP, BLK), F32), vm((NY, 8, BLK), F32), vm((NZ, 16, HEADS), BF16),
        vm((VIEWS, BLK), F32), vm((MP, 40, 128), F32), vm((MP, 8, 256), F32), vm((2, 1, D), F32),
        vm((MP, 8, 128), F32), vm((128, 128), F32), vm((2, SEQ, 128), F32), vm((2, SEQ, 128), F32),
        vm((NZ, 2, PAYH, HEADS), I16), vm((NZ, 2, PAYH, HEADS), I16),
        vm((NZ, 2, PAY, HEADS), I16), vm((NZ, 2, PAY, HEADS), I16),
        vm((2, PAYH, HEADS), I16), vm((2, PAYH, HEADS), I16),
        vm((NZ, PAY, HEADS), I16), vm((NZ, PAY, HEADS), I16),
        sems((3,)), sems((2,)), sems((NZ,)),
        sems((NZ, 8)), sems((NZ, 8)), sems((NY - 1,)), sems((NY,)), sems((4, 2)), sems((4, 2)),
        sems((MP - 1,)), sems((MP,)), sems((NY - 1,)), sems((NY,)), sems((NZ - 1,)), sems((NZ,)),
        sems((MP - 1,)), sems((MP,)), sems((MP - 1,)), sems((MP,)), sems((MP - 1,)), sems((MP,)),
        sems((NZ, 2)), sems((NZ, 2)), sems((NZ, 2)), sems((NZ, 2)),
        sems((2,)), sems((2,)), sems((NZ,)), sems((NZ,)),
    ]
    context_grad, weight_grad, stream_grad = pl.pallas_call(
        kernel,
        out_shape=(
            jax.ShapeDtypeStruct(context.shape, BF16),
            jax.ShapeDtypeStruct((PART, HEADS), F32),
            jax.ShapeDtypeStruct(stream.shape, BF16),
        ),
        in_specs=[
            anywhere, anywhere, anywhere,
            pl.BlockSpec(memory_space=pltpu.VMEM),
            pl.BlockSpec(memory_space=pltpu.SMEM),
        ],
        out_specs=[anywhere] * 3,
        scratch_shapes=scratch,
        compiler_params=pltpu.CompilerParams(
            collective_id=0, has_side_effects=True, vmem_limit_bytes=60 * 2**20
        ),
        cost_estimate=pl.CostEstimate(flops=10**10, bytes_accessed=6 * 10**6, transcendentals=0),
    )(context, w_out.T, stream, gain.reshape(MP, BLK), partner)
    return context_grad, weight_grad.T, stream_grad


def solution(mesh):
    placed = (P("dp", None, "mp"), P("mp", "dp"), P("dp", "mp", None), P(), P())
    return jax.shard_map(
        local,
        mesh=mesh,
        in_specs=placed,
        out_specs=(P("dp", None, "mp"), P("mp", "dp"), P("dp", "mp", None)),
        check_vma=False,
    )
```

time: 646 us -> 120 us (0.19)
  waiting for transfers between devices: 510 us -> 0 us
  Pallas kernels: 0 us -> 113 us
  blocking collectives: 83.1 us -> 0 us
  matrix products: 27.7 us -> 0 us
  between operations: 14.5 us -> 0.65 us
  other arithmetic: 6.58 us -> 0 us
    reduce_scatter x1 -> x0, waiting for transfers between devices: 222 us -> none  [local(): lax.psum_scatter(weight_acc, 'dp', scatter_dimension=1, tiled=True)]
    unnamed x5 -> x0, waiting for transfers between devices: 146 us -> none
    all_gather x2 -> x0, waiting for transfers between devices: 141 us -> none  [the longest x1 73.8 us: local(): weights = lax.all_gather(w_out, 'dp', axis=1, tiled=True)]
    pallas_call x0 -> x1, Pallas kernels: none -> 113 us  [local(): pl.pallas_call(kernel, out_shape=(jax.ShapeDtypeStruct(context.shape, BF1...]
    all_gather x1 -> x0, blocking collectives: 57 us -> none  [local(): gathered = lax.all_gather(emb, 'dp', axis=0, tiled=True)]
    dot_general x5 -> x0, matrix products: 27.7 us -> none  [the longest x1 11.9 us: local(): jnp.einsum('esh,esd->hd', context, piece, preferred_element_type=jnp.floa...]
    psum x1 -> x0, blocking collectives: 26.1 us -> none  [local(): pooled = lax.psum(jnp.sum(values * rstd * gain, axis=1), 'mp') / seq_all]
  transfers between devices with their start and end apart: 4 -> 0, of which waited for: 4 -> 0; matrix products, arithmetic and copies ran while one was open for 4% -> 0% of each run, Pallas kernels for 0% -> 0%
where the time goes in v1:
time: 120 us
  Pallas kernels  113 us (94%)
  local copies, waits for them, and re-layouts  6.4 us (5%)
    pallas_call x1, Pallas kernels, local(): pl.pallas_call(kernel, out_shape=(jax.ShapeDtypeStruct(context.shape, BF1...  113 us
    unnamed x5, local copies, waits for them, and re-layouts  5.05 us

profile of v1, /device:TPU:8, one launch (start us, length us, event | category | flops | bytes accessed | tf_op | source)
XLA Modules:
  0.0 119.8 jit_solution(6128083420395162722)
XLA Ops:
  0.6 1.4 %reshape.9.gain_ref = f32[8,768]{1,0:T(8,128)} reshape(f32[6144]{0:T(1024)} %param.8) | data formatting | bytes 49152 | tf_op jit(solution)/shard_map/reshape | solution.py:598
  2.0 112.8 %shard_map.76 = (bf16[2,512,384]{2,1,0:T(8,128)(2,1)}, f32[192,384]{1,0:T(8,128)}, bf16[2,64,6144]{2,1,0:T(8,128)(2,1)}) custom-call(bf16[2,512,384]{2,1,0:T(8,128)(2,1)} %ctx_hbm.1, bf16[192,384]{1,0:T(8,128)(2,1)} %bitcast.3, bf16[2,64,6144]{2,1,0:T(8,128)(2,1)} %stream_hbm.1, f32[8,768]{1,0:T(8,128)} %reshape.9.gain_ref, s32[64]{0:T(128)} %partner_ref.1), custom_call_target="tpu_custom_call" | custom-call | flops 10000000000 | bytes 6000000 | tf_op jit(solution)/shard_map/pallas_call | solution.py:580
  114.8 0.0 copy-start
  114.8 2.2 %copy.11 = bf16[2,512,384]{2,1,0:T(8,128)(2,1)} copy(bf16[2,512,384]{2,1,0:T(8,128)(2,1)} %get-tuple-element.12) | data formatting | bytes 1572864
  117.0 1.7 %copy.12 = f32[384,192]{0,1:T(8,128)} copy(f32[384,192]{0,1:T(8,128)} %bitcast.2) | data formatting | bytes 589824
  118.7 0.0 copy-done
  118.7 1.1 copy.13
Async XLA Ops:
  114.8 3.9 %copy-start = (bf16[2,64,6144]{2,1,0:T(8,128)(2,1)S(1)}, bf16[2,64,6144]{2,1,0:T(8,128)(2,1)}, u32[]{:S(2)}) copy-start(bf16[2,64,6144]{2,1,0:T(8,128)(2,1)} %get-tuple-element.14) | copy-start | bytes 4718596

commit v2 on v1

--- a/solution.py
+++ b/solution.py
@@ -263,6 +263,7 @@
         wy_wait(d)
     for t in range(2):
         wz_copy(0, t).start()
+    x_forward(0)
     x_send(2)
     for d in range(1, NZ):
         s = lax.rem(z + d, NZ)
@@ -283,7 +284,8 @@
     LB[mp, pl.ds(32, 8), pl.ds(0, 64)] = cross
     LB[mp, pl.ds(32, 8), pl.ds(64, 64)] = jnp.zeros((8, 64), F32)
     ex_send(LB, el_s, el_r)
-    x_forward(0)
+    x_forward(1)
+    x_opposite(0)
     x_send(3)
     ex_wait(LB, el_s, el_r)
     summed = LB[0]
@@ -315,8 +317,8 @@
         for c in range(3):
             UPM[mp, pl.ds(3 * v + c, 1), :] = up8[v : v + 1, 256 * c : 256 * (c + 1)]
     ex_send(UPM, eu_s, eu_r)
-    x_opposite(0)
-    x_forward(1)
+    x_forward(2)
+    x_opposite(1)
     x_send(4)
     ex_wait(UPM, eu_s, eu_r)
     for s in range(MP):
@@ -337,6 +339,9 @@
             line = jnp.sum(jnp.where(diag, column, 0.0), axis=0, keepdims=True)
             TM[mp, pl.ds(r, 1), pl.ds(v * OWN, OWN)] = line
     ex_send(TM, et_s, et_r)
+    x_forward(3)
+    x_opposite(2)
+    x_send(5)
     load_ctx.wait()
     CG[...] = jnp.zeros_like(CG)
     ex_wait(TM, et_s, et_r)
@@ -393,16 +398,9 @@
         sgout(k).start()
         keep = lax.rem(k, 3)
 
-        def matmul(m, carry):
-            c = pl.ds(pl.multiple_of(first + m * 256, 256), 256)
-            left = SG[:, :, c].reshape(2 * SEQ, 256)
-            right = CTX[...].reshape(2 * SEQ, HEADS)
-            PB[keep, pl.ds(pl.multiple_of(m * 256, 256), 256), :] = lax.dot_general(
-                left, right, (((0,), (0,)), ((), ())), preferred_element_type=F32
-            )
-            return carry
-
-        lax.fori_loop(0, 3, matmul, 0)
+        left = SG[:, :, pl.ds(pl.multiple_of(first, BLK), BLK)].reshape(2 * SEQ, BLK)
+        right = CTX[...].reshape(2 * SEQ, HEADS)
+        PB[keep] = lax.dot_general(left, right, (((0,), (0,)), ((), ())), preferred_element_type=F32)
         for h in range(2):
             put(YS0.at[k, h], PB[keep, half_rows(2, h), :], HALF)
             ys0(k, h).start()
@@ -455,28 +453,23 @@
     def project(b):
         first = zblock(b) * BLK
 
-        def step(m, carry):
-            v = lax.div(m, 2)
-            r = pl.ds(pl.multiple_of(lax.rem(m, 2) * 256, 256), 256)
-            left = SG[v, r, pl.ds(pl.multiple_of(first, BLK), BLK)]
-            right = WT[pl.ds(pl.multiple_of(first, BLK), BLK), :]
-            CG[v, r, :] = CG[v, r, :] + jnp.dot(left, right, preferred_element_type=F32)
-            return carry
-
-        lax.fori_loop(0, 4, step, 0)
+        left = SG[:, :, pl.ds(pl.multiple_of(first, BLK), BLK)].reshape(2 * SEQ, BLK)
+        right = WT[pl.ds(pl.multiple_of(first, BLK), BLK), :]
+        update = jnp.dot(left, right, preferred_element_type=F32)
+        CG[...] = CG[...] + update.reshape(2, SEQ, HEADS)
 
     def iteration(k, carry):
-        @pl.when(k <= 2)
-        def _():
-            x_send(k + 5)
-
-        @pl.when(k <= 5)
-        def _():
-            x_forward(k + 2)
-
-        @pl.when(k <= 6)
-        def _():
-            x_opposite(k + 1)
+        @pl.when(k <= 1)
+        def _():
+            x_send(k + 6)
+
+        @pl.when(k <= 3)
+        def _():
+            x_forward(k + 4)
+
+        @pl.when(k <= 4)
+        def _():
+            x_opposite(k + 3)
 
         for f in range(1, 4):
             @pl.when(k == 2 * f - 2)
@@ -554,6 +547,16 @@
         ex(TM, et_s, et_r, d).wait_send()
     pltpu.make_async_copy(CGO, cg_hbm, out_sem.at[0]).wait()
     wg_out.wait()
+
+
+def copy_out(cg, wg, sg, cg_out, wg_out, sg_out, sem):
+    copies = [pltpu.make_async_copy(sg.at[v], sg_out.at[v], sem.at[v]) for v in range(2)]
+    copies += [pltpu.make_async_copy(cg.at[v], cg_out.at[v], sem.at[2 + v]) for v in range(2)]
+    copies.append(pltpu.make_async_copy(wg, wg_out, sem.at[4]))
+    for c in copies:
+        c.start()
+    for c in copies:
+        c.wait()
 
 
 def local(context, w_out, stream, gain, partner):
@@ -596,6 +599,13 @@
         ),
         cost_estimate=pl.CostEstimate(flops=10**10, bytes_accessed=6 * 10**6, transcendentals=0),
     )(context, w_out.T, stream, gain.reshape(MP, BLK), partner)
+    context_grad, weight_grad, stream_grad = pl.pallas_call(
+        copy_out,
+        out_shape=tuple(jax.ShapeDtypeStruct(a.shape, a.dtype) for a in (context_grad, weight_grad, stream_grad)),
+        in_specs=[anywhere] * 3,
+        out_specs=[anywhere] * 3,
+        scratch_shapes=[sems((5,))],
+    )(context_grad, weight_grad, stream_grad)
     return context_grad, weight_grad.T, stream_grad
 
 

time: 120 us -> 199 us (1.66)
  Pallas kernels: 113 us -> 197 us
  local copies, waits for them, and re-layouts: 6.4 us -> 1.35 us
    pallas_call x0 -> x1, Pallas kernels: none -> 81.6 us  [local(): pl.pallas_call(copy_out, out_shape=tuple((jax.ShapeDtypeStruct(a.shape, a...]
    unnamed x5 -> x0, local copies, waits for them, and re-layouts: 5.05 us -> none
    pallas_call x1, Pallas kernels: 113 us -> 115 us  [local(): pl.pallas_call(kernel, out_shape=(jax.ShapeDtypeStruct(context.shape, BF1...]
where the time goes in v2:
time: 199 us
  Pallas kernels  197 us (99%)
    pallas_call x1, Pallas kernels, local(): pl.pallas_call(kernel, out_shape=(jax.ShapeDtypeStruct(context.shape, BF1...  115 us
    pallas_call x1, Pallas kernels, local(): pl.pallas_call(copy_out, out_shape=tuple((jax.ShapeDtypeStruct(a.shape, a...  81.6 us

profile of v2, /device:TPU:8, one launch (start us, length us, event | category | flops | bytes accessed | tf_op | source)
XLA Modules:
  0.0 198.6 jit_solution(14635707668656008366)
XLA Ops:
  0.6 1.4 reshape.9.gain_ref
  2.0 115.1 %shard_map.76 = (bf16[2,512,384]{2,1,0:T(8,128)(2,1)}, f32[192,384]{1,0:T(8,128)}, bf16[2,64,6144]{2,1,0:T(8,128)(2,1)}) custom-call(bf16[2,512,384]{2,1,0:T(8,128)(2,1)} %ctx_hbm.1, bf16[192,384]{1,0:T(8,128)(2,1)} %bitcast.3, bf16[2,64,6144]{2,1,0:T(8,128)(2,1)} %stream_hbm.1, f32[8,768]{1,0:T(8,128)} %reshape.9.gain_ref, s32[64]{0:T(128)} %partner_ref.1), custom_call_target="tpu_custom_call" | custom-call | flops 10000000000 | bytes 6000000 | tf_op jit(solution)/shard_map/pallas_call | solution.py:583
  117.1 81.6 %shard_map.77 = (bf16[2,512,384]{2,1,0:T(8,128)(2,1)}, f32[192,384]{1,0:T(8,128)}, bf16[2,64,6144]{2,1,0:T(8,128)(2,1)}) custom-call(bf16[2,512,384]{2,1,0:T(8,128)(2,1)} %get-tuple-element.9.cg, f32[192,384]{1,0:T(8,128)} %get-tuple-element.10.wg, bf16[2,64,6144]{2,1,0:T(8,128)(2,1)} %get-tuple-element.11.sg), custom_call_target="tpu_custom_call" | custom-call | tf_op jit(solution)/shard_map/pallas_call | solution.py:602

commit v3 on v2

--- a/solution.py
+++ b/solution.py
@@ -20,6 +20,8 @@
 HALF = PART // 2
 PAY = PART + 16
 PAYH = HALF + 16
+WIDE = 256
+THIN = HEADS - WIDE
 F32 = jnp.float32
 BF16 = jnp.bfloat16
 I16 = jnp.int16
@@ -30,7 +32,7 @@
     top = jnp.max(jnp.abs(values), axis=0, keepdims=True)
     expo = jnp.ceil(16.0 * jnp.log2(jnp.maximum(top, 1e-30)))
     whole = jnp.round(values * jnp.exp2(14.9 - expo * 0.0625)).astype(jnp.int32).astype(I16)
-    tail = jnp.broadcast_to(expo, (16, HEADS)).astype(jnp.int32).astype(I16)
+    tail = jnp.broadcast_to(expo, (16, values.shape[1])).astype(jnp.int32).astype(I16)
     return whole, tail
 
 
@@ -51,10 +53,13 @@
     G, SG, WT, CTX, CG, CGO, PB, WGO,
     EX1, UN, YB, ZB, E, LB, UPM, UPF, TM, TT, RB, CB,
     YS0, YR0, YS1, YR1, ZS0, ZR0, ZS1, ZR1,
+    BZS0, BZR0, BZS1, BZR1, BYS0, BYR0, BYS1, BYR1,
     in_sem, out_sem, sgo_sem,
     xs_s, x_r, wy_s, wy_r, wz_s, wz_r,
     e1_s, e1_r, ey_s, ey_r, ez_s, ez_r, el_s, el_r, eu_s, eu_r, et_s, et_r,
     ys0_s, ys0_r, ys1_s, ys1_r, zs0_s, zs0_r, zs1_s, zs1_r,
+    bz0_s, bz0_r, bz1_s, bz1_r, by0_s, by0_r, by1_s, by1_r,
+    vz_s, vz_r, vw_s, vw_r, vy_s, vy_r,
 ):
     dp = lax.axis_index("dp")
     mp = lax.axis_index("mp")
@@ -81,7 +86,7 @@
     load_stream = pltpu.make_async_copy(stream_hbm, G.at[:, own_rows, :], in_sem.at[0])
     load_ctx = pltpu.make_async_copy(ctx_hbm, CTX, in_sem.at[1])
     load_w = pltpu.make_async_copy(
-        w_hbm, WT.at[pl.ds(pl.multiple_of(dp * PART, PART), PART), :], in_sem.at[2]
+        w_hbm, WT.at[z, y], in_sem.at[2]
     )
     load_stream.start()
     load_w.start()
@@ -153,19 +158,18 @@
             x_wait(k, t)
 
     def wy_copy(d):
-        ref = WT.at[pl.ds(pl.multiple_of(dp * PART, PART), PART), :]
+        ref = WT.at[z, y, pl.ds(0, HALF), :]
         return remote(ref, ref, wy_s.at[d - 1], wy_r.at[y], near(dy=d))
 
     def wy_wait(d):
         s = lax.rem(y + d, NY)
-        ref = WT.at[pl.ds(pl.multiple_of((z * NY + s) * PART, PART), PART), :]
+        ref = WT.at[z, s, pl.ds(0, HALF), :]
         remote(ref, ref, wy_s.at[d - 1], wy_r.at[s], near(dy=d)).wait_recv()
 
     def wz_ref(bundle, f, t):
-        start = pl.multiple_of(bundle * BLK, BLK)
         if f == 3:
-            return WT.at[pl.ds(pl.multiple_of(start + t * (BLK // 2), BLK // 2), BLK // 2), :]
-        return WT.at[pl.ds(start, BLK), :]
+            return WT.at[bundle, pl.ds(2 * t, 2), pl.ds(0, HALF), :]
+        return WT.at[bundle, :, pl.ds(0, HALF), :]
 
     def wz_copy(f, t):
         step = f if t else NZ - f
@@ -176,6 +180,65 @@
         step = f + 1 if t else NZ - f - 1
         ref = wz_ref(lax.rem(z + step, NZ), f, t)
         remote(ref, ref, wz_s.at[f, t], wz_r.at[f, t], near(dz=1)).wait_recv()
+
+    def vz_ref(bundle, f, t):
+        if f == 3:
+            return WT.at[bundle, y, pl.ds(HALF + t * (HALF // 2), HALF // 2), :]
+        return WT.at[bundle, y, pl.ds(HALF, HALF), :]
+
+    def vz_copy(f, t):
+        step = f if t else NZ - f
+        ref = vz_ref(lax.rem(z + step, NZ), f, t)
+        return remote(ref, ref, vz_s.at[f, t], vz_r.at[f, t], near(dz=-1 if t else 1))
+
+    def vz_wait(f, t):
+        step = f + 1 if t else NZ - f - 1
+        ref = vz_ref(lax.rem(z + step, NZ), f, t)
+        remote(ref, ref, vz_s.at[f, t], vz_r.at[f, t], near(dz=1)).wait_recv()
+
+    def vw_ref(n, dy):
+        return WT.at[lax.rem(z + NZ - n, NZ), lax.rem(y + NY + dy, NY), pl.ds(HALF, HALF), :]
+
+    def vw_copy(n, t):
+        ref = vw_ref(n, 0)
+        return remote(ref, ref, vw_s.at[n, t], vw_r.at[n, t], near(dy=-1 if t else 1))
+
+    def vw_wait(n, t):
+        ref = vw_ref(n, 1 if t else -1)
+        remote(ref, ref, vw_s.at[n, t], vw_r.at[n, t], near(dy=1)).wait_recv()
+
+    def vw_send(n):
+        for t in range(2):
+            vw_copy(n, t).start()
+
+    def vz_next(f):
+        for t in range(2):
+            vz_wait(f - 1, t)
+            vz_copy(f, t).start()
+            vw_send(NZ - f if t else f)
+
+    def vy_ref(dy, part):
+        s = lax.rem(y + NY + dy, NY)
+        return WT.at[pl.ds(part * (NZ // 2), NZ // 2), s, pl.ds(HALF, HALF), :]
+
+    def vy_copy(t):
+        ref = vy_ref(1 if t else -1, t)
+        return remote(ref, ref, vy_s.at[t], vy_r.at[t], near(dy=-1 if t else 1))
+
+    def vy_wait(t):
+        ref = vy_ref(2, t)
+        remote(ref, ref, vy_s.at[t], vy_r.at[t], near(dy=1)).wait_recv()
+
+    def vy_begin():
+        for t in range(2):
+            vz_wait(3, t)
+        vw_send(NZ // 2)
+
+    def vy_next():
+        for t in range(2):
+            for n in range(NZ):
+                vw_wait(n, t)
+            vy_copy(t).start()
 
     def wz_next(f):
         for t in range(2):
@@ -225,6 +288,9 @@
     load_w.wait()
     for d in (2, 1, 3):
         wy_copy(d).start()
+    for t in range(2):
+        vz_copy(0, t).start()
+    vw_send(0)
     x_send(0)
     x_send(1)
     ex_wait(EX1, e1_s, e1_r)
@@ -259,6 +325,7 @@
     ZB[z] = jnp.concatenate([eight[:, 0:HEADS], eight[:, HEADS:BLK]], axis=0).astype(BF16)
     for d in (4, 3, 5, 2, 6, 1, 7):
         ez_copy(d).start()
+    vz_next(1)
     for d in range(1, NY):
         wy_wait(d)
     for t in range(2):
@@ -284,6 +351,8 @@
     LB[mp, pl.ds(32, 8), pl.ds(0, 64)] = cross
     LB[mp, pl.ds(32, 8), pl.ds(64, 64)] = jnp.zeros((8, 64), F32)
     ex_send(LB, el_s, el_r)
+    vz_next(2)
+    wz_next(1)
     x_forward(1)
     x_opposite(0)
     x_send(3)
@@ -320,6 +389,7 @@
     x_forward(2)
     x_opposite(1)
     x_send(4)
+    vz_next(3)
     ex_wait(UPM, eu_s, eu_r)
     for s in range(MP):
         for v in range(2):
@@ -339,6 +409,8 @@
             line = jnp.sum(jnp.where(diag, column, 0.0), axis=0, keepdims=True)
             TM[mp, pl.ds(r, 1), pl.ds(v * OWN, OWN)] = line
     ex_send(TM, et_s, et_r)
+    vy_begin()
+    wz_next(2)
     x_forward(3)
     x_opposite(2)
     x_send(5)
@@ -355,6 +427,8 @@
             RB[v, pl.ds(s * OWN, OWN), :] = jnp.broadcast_to(piece[:, 8 * s : 8 * s + 1], (OWN, 128))
             CB[v, pl.ds(s * OWN, OWN), :] = jnp.broadcast_to(piece[:, 8 * s + 1 : 8 * s + 2], (OWN, 128))
 
+    wide, thin = pl.ds(0, WIDE), pl.ds(WIDE, THIN)
+
     def part_rows(dy):
         return pl.ds(pl.multiple_of(lax.rem(y + dy, NY) * PART, PART), PART)
 
@@ -396,35 +470,35 @@
 
         lax.fori_loop(0, 2 * MP, build, 0)
         sgout(k).start()
-        keep = lax.rem(k, 3)
+        keep = lax.rem(k, 5)
 
         left = SG[:, :, pl.ds(pl.multiple_of(first, BLK), BLK)].reshape(2 * SEQ, BLK)
         right = CTX[...].reshape(2 * SEQ, HEADS)
         PB[keep] = lax.dot_general(left, right, (((0,), (0,)), ((), ())), preferred_element_type=F32)
         for h in range(2):
-            put(YS0.at[k, h], PB[keep, half_rows(2, h), :], HALF)
+            put(YS0.at[k, h], PB[keep, half_rows(2, h), wide], HALF)
             ys0(k, h).start()
 
     def y_second(k):
-        keep = lax.rem(k, 3)
+        keep = lax.rem(k, 5)
         for h in range(2):
             ys0(k, h).wait_recv()
             spot = half_rows(1 if h == 0 else 3, h)
-            PB[keep, spot, :] = PB[keep, spot, :] + decode(YR0.at[k, h], HALF)
-            put(YS1.at[k, h], PB[keep, part_rows(1 if h == 0 else 3), :], PART)
+            PB[keep, spot, wide] = PB[keep, spot, wide] + decode(YR0.at[k, h], HALF)
+            put(YS1.at[k, h], PB[keep, part_rows(1 if h == 0 else 3), wide], PART)
             ys1(k, h).start()
 
     def z_part(k):
-        keep = lax.rem(k, 3)
+        keep = lax.rem(k, 5)
         ys1(k, 0).wait_recv()
         ys1(k, 1).wait_recv()
         spot = part_rows(0)
-        PB[keep, spot, :] = PB[keep, spot, :] + decode(YR1.at[k, 0], PART) + decode(YR1.at[k, 1], PART)
+        PB[keep, spot, wide] = PB[keep, spot, wide] + decode(YR1.at[k, 0], PART) + decode(YR1.at[k, 1], PART)
 
         @pl.when(k == 0)
         def _():
             for h in range(2):
-                put(ZS0.at[h], PB[keep, half_rows(0, h), :], HALF)
+                put(ZS0.at[h], PB[keep, half_rows(0, h), wide], HALF)
                 zs0(h).start()
 
         for h in range(2):
@@ -432,29 +506,91 @@
             def _():
                 zs0(h).wait_recv()
                 half = half_rows(0, h)
-                PB[keep, half, :] = PB[keep, half, :] + decode(ZR0.at[h], HALF)
+                PB[keep, half, wide] = PB[keep, half, wide] + decode(ZR0.at[h], HALF)
 
         @pl.when(jnp.logical_and(k >= 3, k <= 6))
         def _():
             zs1(k - 2).wait_recv()
-            PB[keep, spot, :] = PB[keep, spot, :] + decode(ZR1.at[k - 2], PART)
+            PB[keep, spot, wide] = PB[keep, spot, wide] + decode(ZR1.at[k - 2], PART)
 
         @pl.when(jnp.logical_and(k >= 1, k <= 6))
         def _():
-            put(ZS1.at[k], PB[keep, spot, :], PART)
+            put(ZS1.at[k], PB[keep, spot, wide], PART)
             zs1(k).start()
 
         @pl.when(k == 7)
         def _():
             zs1(5).wait_recv()
             zs1(6).wait_recv()
-            WGO[...] = PB[keep, spot, :] + decode(ZR1.at[5], PART) + decode(ZR1.at[6], PART)
+            WGO[:, wide] = PB[keep, spot, wide] + decode(ZR1.at[5], PART) + decode(ZR1.at[6], PART)
+
+    def bz0(h):
+        return remote(BZS0.at[h], BZR0.at[h], bz0_s.at[h], bz0_r.at[h], near(dz=1 if h == 0 else -1))
+
+    def bz1(k):
+        odd = lax.rem(k, 2)
+        target = lax.rem(z + NZ - 1 + 2 * odd, NZ) * NY + y
+        return remote(BZS1.at[k], BZR1.at[k], bz1_s.at[k], bz1_r.at[k], (target, mp))
+
+    def by0(h):
+        return remote(BYS0.at[h], BYR0.at[h], by0_s.at[h], by0_r.at[h], near(dy=1 if h == 0 else -1))
+
+    def by1(h):
+        return remote(BYS1.at[h], BYR1.at[h], by1_s.at[h], by1_r.at[h], near(dy=1 if h == 0 else -1))
+
+    def b_part(k):
+        keep = lax.rem(k, 5)
+
+        @pl.when(k == 0)
+        def _():
+            for h in range(2):
+                put(BZS0.at[h], PB[keep, pl.ds(h * BLK // 2, BLK // 2), thin], BLK // 2)
+                bz0(h).start()
+
+        for h in range(2):
+            @pl.when(k == 1 + h)
+            def _():
+                bz0(h).wait_recv()
+                half = pl.ds(h * BLK // 2, BLK // 2)
+                PB[keep, half, thin] = PB[keep, half, thin] + decode(BZR0.at[h], BLK // 2)
+
+        @pl.when(jnp.logical_and(k >= 3, k <= 6))
+        def _():
+            bz1(k - 2).wait_recv()
+            PB[keep, :, thin] = PB[keep, :, thin] + decode(BZR1.at[k - 2], BLK)
+
+        @pl.when(jnp.logical_and(k >= 1, k <= 6))
+        def _():
+            put(BZS1.at[k], PB[keep, :, thin], BLK)
+            bz1(k).start()
+
+        @pl.when(k == 7)
+        def _():
+            bz1(5).wait_recv()
+            bz1(6).wait_recv()
+            PB[keep, :, thin] = PB[keep, :, thin] + decode(BZR1.at[5], BLK) + decode(BZR1.at[6], BLK)
+            for h in range(2):
+                put(BYS0.at[h], PB[keep, half_rows(2, h), thin], HALF)
+                by0(h).start()
+
+    def b_second():
+        for h in range(2):
+            by0(h).wait_recv()
+            spot = half_rows(1 if h == 0 else 3, h)
+            PB[2, spot, thin] = PB[2, spot, thin] + decode(BYR0.at[h], HALF)
+            put(BYS1.at[h], PB[2, part_rows(1 if h == 0 else 3), thin], PART)
+            by1(h).start()
+
+    def b_last():
+        by1(0).wait_recv()
+        by1(1).wait_recv()
+        WGO[:, thin] = PB[2, part_rows(0), thin] + decode(BYR1.at[0], PART) + decode(BYR1.at[1], PART)
 
     def project(b):
         first = zblock(b) * BLK
 
         left = SG[:, :, pl.ds(pl.multiple_of(first, BLK), BLK)].reshape(2 * SEQ, BLK)
-        right = WT[pl.ds(pl.multiple_of(first, BLK), BLK), :]
+        right = WT[zblock(b)].reshape(BLK, HEADS)
         update = jnp.dot(left, right, preferred_element_type=F32)
         CG[...] = CG[...] + update.reshape(2, SEQ, HEADS)
 
@@ -471,10 +607,19 @@
         def _():
             x_opposite(k + 3)
 
-        for f in range(1, 4):
-            @pl.when(k == 2 * f - 2)
-            def _():
-                wz_next(f)
+        @pl.when(k == 1)
+        def _():
+            wz_next(3)
+
+        @pl.when(k == 0)
+        def _():
+            vy_next()
+
+        @pl.when(k == 4)
+        def _():
+            for t in range(2):
+                wz_wait(3, t)
+                vy_wait(t)
 
         @pl.when(k <= 7)
         def _():
@@ -482,11 +627,15 @@
 
         @pl.when(jnp.logical_and(k >= 1, k <= 8))
         def _():
-            y_second(k - 1)
-
-        @pl.when(k >= 2)
-        def _():
-            z_part(k - 2)
+            b_part(k - 1)
+
+        @pl.when(jnp.logical_and(k >= 2, k <= 9))
+        def _():
+            y_second(k - 2)
+
+        @pl.when(k >= 4)
+        def _():
+            z_part(k - 4)
 
         @pl.when(jnp.logical_and(k >= 4, k <= 5))
         def _():
@@ -500,16 +649,19 @@
         def _():
             project(5)
             project(6)
+
+        @pl.when(k == 9)
+        def _():
+            b_second()
             project(7)
-            wz_wait(3, 0)
-            wz_wait(3, 1)
             project(0)
             CGO[...] = CG[...].astype(BF16)
             pltpu.make_async_copy(CGO, cg_hbm, out_sem.at[0]).start()
 
         return carry
 
-    lax.fori_loop(0, 10, iteration, 0)
+    lax.fori_loop(0, 12, iteration, 0)
+    b_last()
     wg_out = pltpu.make_async_copy(WGO, wg_hbm, out_sem.at[1])
     wg_out.start()
 
@@ -526,18 +678,26 @@
         @pl.when(jnp.logical_and(k >= 1, k <= 6))
         def _():
             zs1(k).wait_send()
+            bz1(k).wait_send()
 
         return carry
 
     lax.fori_loop(0, NZ, drain, 0)
     for h in range(2):
         zs0(h).wait_send()
+        bz0(h).wait_send()
+        by0(h).wait_send()
+        by1(h).wait_send()
+        vy_copy(h).wait_send()
+        for n in range(NZ):
+            vw_copy(n, h).wait_send()
     for d in range(1, NY):
         wy_copy(d).wait_send()
         ey_copy(d).wait_send()
     for f in range(4):
         for t in range(2):
             wz_copy(f, t).wait_send()
+            vz_copy(f, t).wait_send()
     for d in range(1, NZ):
         ez_copy(d).wait_send()
     for d in range(1, MP):
@@ -549,14 +709,18 @@
     wg_out.wait()
 
 
-def copy_out(cg, wg, sg, cg_out, wg_out, sg_out, sem):
-    copies = [pltpu.make_async_copy(sg.at[v], sg_out.at[v], sem.at[v]) for v in range(2)]
-    copies += [pltpu.make_async_copy(cg.at[v], cg_out.at[v], sem.at[2 + v]) for v in range(2)]
-    copies.append(pltpu.make_async_copy(wg, wg_out, sem.at[4]))
-    for c in copies:
-        c.start()
-    for c in copies:
-        c.wait()
+def copy_out(cg, wg, sg, cg_out, wg_out, sg_out, cg_mid, wg_mid, sg_mid, sem_in, sem_out):
+    moves = [(sg, sg_mid, sg_out, v) for v in range(2)] + [(cg, cg_mid, cg_out, v) for v in range(2)]
+    moves = [(a.at[v], b.at[v], c.at[v]) for a, b, c, v in moves] + [(wg, wg_mid, wg_out)]
+    loads = [pltpu.make_async_copy(a, b, sem_in.at[n]) for n, (a, b, c) in enumerate(moves)]
+    stores = [pltpu.make_async_copy(b, c, sem_out.at[n]) for n, (a, b, c) in enumerate(moves)]
+    for load in loads:
+        load.start()
+    for load, store in zip(loads, stores):
+        load.wait()
+        store.start()
+    for store in stores:
+        store.wait()
 
 
 def local(context, w_out, stream, gain, partner):
@@ -564,21 +728,26 @@
     sems = pltpu.SemaphoreType.DMA
     vm = pltpu.VMEM
     scratch = [
-        vm((2, SEQ, D), BF16), vm((2, SEQ, D), BF16), vm((D, HEADS), BF16), vm((2, SEQ, HEADS), BF16),
-        vm((2, SEQ, HEADS), F32), vm((2, SEQ, HEADS), BF16), vm((3, BLK, HEADS), F32), vm((PART, HEADS), F32),
+        vm((2, SEQ, D), BF16), vm((2, SEQ, D), BF16), vm((NZ, NY, PART, HEADS), BF16), vm((2, SEQ, HEADS), BF16),
+        vm((2, SEQ, HEADS), F32), vm((2, SEQ, HEADS), BF16), vm((5, BLK, HEADS), F32), vm((PART, HEADS), F32),
         vm((MP, 2, MP, BLK), F32), vm((2, MP, BLK), F32), vm((NY, 8, BLK), F32), vm((NZ, 16, HEADS), BF16),
         vm((VIEWS, BLK), F32), vm((MP, 40, 128), F32), vm((MP, 8, 256), F32), vm((2, 1, D), F32),
         vm((MP, 8, 128), F32), vm((128, 128), F32), vm((2, SEQ, 128), F32), vm((2, SEQ, 128), F32),
-        vm((NZ, 2, PAYH, HEADS), I16), vm((NZ, 2, PAYH, HEADS), I16),
-        vm((NZ, 2, PAY, HEADS), I16), vm((NZ, 2, PAY, HEADS), I16),
-        vm((2, PAYH, HEADS), I16), vm((2, PAYH, HEADS), I16),
-        vm((NZ, PAY, HEADS), I16), vm((NZ, PAY, HEADS), I16),
+        vm((NZ, 2, PAYH, WIDE), I16), vm((NZ, 2, PAYH, WIDE), I16),
+        vm((NZ, 2, PAY, WIDE), I16), vm((NZ, 2, PAY, WIDE), I16),
+        vm((2, PAYH, WIDE), I16), vm((2, PAYH, WIDE), I16),
+        vm((NZ, PAY, WIDE), I16), vm((NZ, PAY, WIDE), I16),
+        vm((2, BLK // 2 + 16, THIN), I16), vm((2, BLK // 2 + 16, THIN), I16),
+        vm((NZ, BLK + 16, THIN), I16), vm((NZ, BLK + 16, THIN), I16),
+        vm((2, PAYH, THIN), I16), vm((2, PAYH, THIN), I16), vm((2, PAY, THIN), I16), vm((2, PAY, THIN), I16),
         sems((3,)), sems((2,)), sems((NZ,)),
         sems((NZ, 8)), sems((NZ, 8)), sems((NY - 1,)), sems((NY,)), sems((4, 2)), sems((4, 2)),
         sems((MP - 1,)), sems((MP,)), sems((NY - 1,)), sems((NY,)), sems((NZ - 1,)), sems((NZ,)),
         sems((MP - 1,)), sems((MP,)), sems((MP - 1,)), sems((MP,)), sems((MP - 1,)), sems((MP,)),
         sems((NZ, 2)), sems((NZ, 2)), sems((NZ, 2)), sems((NZ, 2)),
         sems((2,)), sems((2,)), sems((NZ,)), sems((NZ,)),
+        sems((2,)), sems((2,)), sems((NZ,)), sems((NZ,)), sems((2,)), sems((2,)), sems((2,)), sems((2,)),
+        sems((4, 2)), sems((4, 2)), sems((NZ, 2)), sems((NZ, 2)), sems((2,)), sems((2,)),
     ]
     context_grad, weight_grad, stream_grad = pl.pallas_call(
         kernel,
@@ -604,7 +773,7 @@
         out_shape=tuple(jax.ShapeDtypeStruct(a.shape, a.dtype) for a in (context_grad, weight_grad, stream_grad)),
         in_specs=[anywhere] * 3,
         out_specs=[anywhere] * 3,
-        scratch_shapes=[sems((5,))],
+        scratch_shapes=[vm(context.shape, BF16), vm((PART, HEADS), F32), vm(stream.shape, BF16), sems((5,)), sems((5,))],
     )(context_grad, weight_grad, stream_grad)
     return context_grad, weight_grad.T, stream_grad
 

time: 199 us -> 115 us (0.58)
  Pallas kernels: 197 us -> 113 us
    pallas_call x1, Pallas kernels: 81.6 us -> 2.71 us  [local(): pl.pallas_call(copy_out, out_shape=tuple((jax.ShapeDtypeStruct(a.shape, a...]
    pallas_call x1, Pallas kernels: 115 us -> 110 us  [local(): pl.pallas_call(kernel, out_shape=(jax.ShapeDtypeStruct(context.shape, BF1...]
where the time goes in v3:
time: 115 us
  Pallas kernels  113 us (98%)
  local copies, waits for them, and re-layouts  1.35 us (1%)
    pallas_call x1, Pallas kernels, local(): pl.pallas_call(kernel, out_shape=(jax.ShapeDtypeStruct(context.shape, BF1...  110 us
    pallas_call x1, Pallas kernels, local(): pl.pallas_call(copy_out, out_shape=tuple((jax.ShapeDtypeStruct(a.shape, a...  2.71 us

profile of v3, /device:TPU:8, one launch (start us, length us, event | category | flops | bytes accessed | tf_op | source)
XLA Modules:
  0.0 114.9 jit_solution(16509448587255574100)
XLA Ops:
  0.6 1.4 %reshape.9.gain_ref = f32[8,768]{1,0:T(8,128)} reshape(f32[6144]{0:T(1024)} %param.8) | data formatting | bytes 49152 | tf_op jit(solution)/shard_map/reshape | solution.py:770
  2.0 110.2 %shard_map.76 = (bf16[2,512,384]{2,1,0:T(8,128)(2,1)}, f32[192,384]{1,0:T(8,128)}, bf16[2,64,6144]{2,1,0:T(8,128)(2,1)}) custom-call(bf16[2,512,384]{2,1,0:T(8,128)(2,1)} %ctx_hbm.1, bf16[192,384]{1,0:T(8,128)(2,1)} %bitcast.3, bf16[2,64,6144]{2,1,0:T(8,128)(2,1)} %stream_hbm.1, f32[8,768]{1,0:T(8,128)} %reshape.9.gain_ref, s32[64]{0:T(128)} %partner_ref.1), custom_call_target="tpu_custom_call" | custom-call | flops 10000000000 | bytes 6000000 | tf_op jit(solution)/shard_map/pallas_call | solution.py:752
  112.2 2.7 %shard_map.77 = (bf16[2,512,384]{2,1,0:T(8,128)(2,1)}, f32[192,384]{1,0:T(8,128)}, bf16[2,64,6144]{2,1,0:T(8,128)(2,1)}) custom-call(bf16[2,512,384]{2,1,0:T(8,128)(2,1)} %get-tuple-element.9.cg, f32[192,384]{1,0:T(8,128)} %get-tuple-element.10.wg, bf16[2,64,6144]{2,1,0:T(8,128)(2,1)} %get-tuple-element.11.sg), custom_call_target="tpu_custom_call" | custom-call | tf_op jit(solution)/shard_map/pallas_call | solution.py:771

commit v4 on v3

--- a/solution.py
+++ b/solution.py
@@ -54,7 +54,7 @@
     EX1, UN, YB, ZB, E, LB, UPM, UPF, TM, TT, RB, CB,
     YS0, YR0, YS1, YR1, ZS0, ZR0, ZS1, ZR1,
     BZS0, BZR0, BZS1, BZR1, BYS0, BYR0, BYS1, BYR1,
-    in_sem, out_sem, sgo_sem,
+    GA, in_sem, out_sem, sgo_sem,
     xs_s, x_r, wy_s, wy_r, wz_s, wz_r,
     e1_s, e1_r, ey_s, ey_r, ez_s, ez_r, el_s, el_r, eu_s, eu_r, et_s, et_r,
     ys0_s, ys0_r, ys1_s, ys1_r, zs0_s, zs0_r, zs1_s, zs1_r,
@@ -295,7 +295,9 @@
     x_send(1)
     ex_wait(EX1, e1_s, e1_r)
 
-    gain8 = gain_ref[...]
+    for q in range(MP):
+        GA[pl.ds(q, 1), :] = gain_ref[pl.ds(q * BLK, BLK)].reshape(1, BLK)
+    gain8 = GA[...]
     squares = []
     for v in range(2):
         total = EX1[0, v]
@@ -380,7 +382,7 @@
     along = SHARP * jnp.sum(coef8 * cross, axis=1, keepdims=True)
     inv8 = two(jnp.broadcast_to(squares[0], (1, BLK)), jnp.broadcast_to(squares[1], (1, BLK)), 0)
     dpooled = inv8 * (demb - unit8 * along)
-    up8 = gain_ref[pl.ds(mp, 1), :] * dpooled * (1.0 / SEQ)
+    up8 = GA[pl.ds(mp, 1), :] * dpooled * (1.0 / SEQ)
     UPM[mp] = jnp.zeros((8, 256), F32)
     for v in range(2):
         for c in range(3):
@@ -740,7 +742,7 @@
         vm((2, BLK // 2 + 16, THIN), I16), vm((2, BLK // 2 + 16, THIN), I16),
         vm((NZ, BLK + 16, THIN), I16), vm((NZ, BLK + 16, THIN), I16),
         vm((2, PAYH, THIN), I16), vm((2, PAYH, THIN), I16), vm((2, PAY, THIN), I16), vm((2, PAY, THIN), I16),
-        sems((3,)), sems((2,)), sems((NZ,)),
+        vm((MP, BLK), F32), sems((3,)), sems((2,)), sems((NZ,)),
         sems((NZ, 8)), sems((NZ, 8)), sems((NY - 1,)), sems((NY,)), sems((4, 2)), sems((4, 2)),
         sems((MP - 1,)), sems((MP,)), sems((NY - 1,)), sems((NY,)), sems((NZ - 1,)), sems((NZ,)),
         sems((MP - 1,)), sems((MP,)), sems((MP - 1,)), sems((MP,)), sems((MP - 1,)), sems((MP,)),
@@ -767,7 +769,7 @@
             collective_id=0, has_side_effects=True, vmem_limit_bytes=60 * 2**20
         ),
         cost_estimate=pl.CostEstimate(flops=10**10, bytes_accessed=6 * 10**6, transcendentals=0),
-    )(context, w_out.T, stream, gain.reshape(MP, BLK), partner)
+    )(context, w_out.T, stream, gain, partner)
     context_grad, weight_grad, stream_grad = pl.pallas_call(
         copy_out,
         out_shape=tuple(jax.ShapeDtypeStruct(a.shape, a.dtype) for a in (context_grad, weight_grad, stream_grad)),

time: 115 us -> 114 us (level)
  local copies, waits for them, and re-layouts: 1.35 us -> 0 us
    reshape x1 -> x0, local copies, waits for them, and re-layouts: 1.35 us -> none  [local(): gain.reshape(MP, BLK)]
where the time goes in v4:
time: 114 us
  Pallas kernels  113 us (99%)
    pallas_call x1, Pallas kernels, local(): pl.pallas_call(kernel, out_shape=(jax.ShapeDtypeStruct(context.shape, BF1...  110 us
    pallas_call x1, Pallas kernels, local(): pl.pallas_call(copy_out, out_shape=tuple((jax.ShapeDtypeStruct(a.shape, a...  2.71 us

profile of v4, /device:TPU:8, one launch (start us, length us, event | category | flops | bytes accessed | tf_op | source)
XLA Modules:
  0.0 113.6 jit_solution(15704426801206690113)
XLA Ops:
  0.6 110.2 %shard_map.76 = (bf16[2,512,384]{2,1,0:T(8,128)(2,1)}, f32[192,384]{1,0:T(8,128)}, bf16[2,64,6144]{2,1,0:T(8,128)(2,1)}) custom-call(bf16[2,512,384]{2,1,0:T(8,128)(2,1)} %ctx_hbm.1, bf16[192,384]{1,0:T(8,128)(2,1)} %bitcast.3, bf16[2,64,6144]{2,1,0:T(8,128)(2,1)} %stream_hbm.1, f32[6144]{0:T(1024)} %gain_ref.1, s32[64]{0:T(128)} %partner_ref.1), custom_call_target="tpu_custom_call" | custom-call | flops 10000000000 | bytes 6000000 | tf_op jit(solution)/shard_map/pallas_call | solution.py:754
  110.9 2.7 %shard_map.77 = (bf16[2,512,384]{2,1,0:T(8,128)(2,1)}, f32[192,384]{1,0:T(8,128)}, bf16[2,64,6144]{2,1,0:T(8,128)(2,1)}) custom-call(bf16[2,512,384]{2,1,0:T(8,128)(2,1)} %get-tuple-element.9.cg, f32[192,384]{1,0:T(8,128)} %get-tuple-element.10.wg, bf16[2,64,6144]{2,1,0:T(8,128)(2,1)} %get-tuple-element.11.sg), custom_call_target="tpu_custom_call" | custom-call | tf_op jit(solution)/shard_map/pallas_call | solution.py:773
